TPU v7x, 32 devices: a whole 2x2x4 slice. The times are simulated.
32 devices in a mesh: dp: 8 (over y, x, core), tensor: 4 (over z).
Axes of the slice: x: 2, y: 2, z: 4, core: 2. Of those that a mesh axis runs over, the one named last changes fastest.
Arguments:
- block_input: bfloat16 [24576, 768], P('dp'), may hold values from -6 to 6
- cotangent: bfloat16 [24576, 768], P('dp'), may hold values from -6 to 6
- heads_weight: bfloat16 [768, 2304], P('dp', 'tensor'), may hold values from -0.21875 to 0.21875
- heads_bias: bfloat16 [2304], P(('tensor', 'dp')), may hold values from -3 to 3
- merge_weight: bfloat16 [768, 768], P('tensor', 'dp'), may hold values from -0.875 to 0.875
- merge_bias: bfloat16 [768], P('dp'), may hold values from -3 to 3
- up_weight: bfloat16 [768, 3072], P('dp', 'tensor'), may hold values from -0.21875 to 0.21875
- up_bias: bfloat16 [3072], P(('tensor', 'dp')), may hold values from -3 to 3
- down_weight: bfloat16 [3072, 768], P('tensor', 'dp'), may hold values from -0.15625 to 0.15625
- down_bias: bfloat16 [768], P('dp'), may hold values from -3 to 3
- first_gain: bfloat16 [768], P('dp'), may hold values from 0.099609375 to 1.8984375
- first_shift: bfloat16 [768], P('dp'), may hold values from -2 to 2
- second_gain: bfloat16 [768], P('dp'), may hold values from 0.099609375 to 1.8984375
- second_shift: bfloat16 [768], P('dp'), may hold values from -2 to 2
Outputs:
- layer_output: bfloat16 [24576, 768], P('dp')
- input_grad: float32 [24576, 768], P('dp')
- heads_weight_grad: float32 [768, 2304], P('dp', 'tensor')
- heads_bias_grad: float32 [2304], P(('tensor', 'dp'))
- merge_weight_grad: float32 [768, 768], P('tensor', 'dp')
- merge_bias_grad: float32 [768], P('dp')
- up_weight_grad: float32 [768, 3072], P('dp', 'tensor')
- up_bias_grad: float32 [3072], P(('tensor', 'dp'))
- down_weight_grad: float32 [3072, 768], P('tensor', 'dp')
- down_bias_grad: float32 [768], P('dp')
- first_gain_grad: float32 [768], P('dp')
- first_shift_grad: float32 [768], P('dp')
- second_gain_grad: float32 [768], P('dp')
- second_shift_grad: float32 [768], P('dp')
All inputs are finite; a program needn't handle non-finite values.
Results may differ from a plain program's by a relative error of at most 0.012.
Values may be sent and summed in bfloat16 or wider, within the bound.
No kernel may reach another device: no remote copies, remote signals or barrier semaphores. Data moves between devices by JAX's collectives and lax.ppermute only.
A program may use at most 192 MiB of HBM per device.

v0:
```python
from functools import partial
import math

import jax
import jax.numpy as jnp
from jax import lax
from jax.sharding import PartitionSpec as P

HD = 64
ROT = 16
SEQ = 512
MB = 2


def layer_norm(values, scale, shift):
    average = jnp.mean(values, axis=-1, keepdims=True)
    centred = values - average
    spread = jnp.mean(centred * centred, axis=-1, keepdims=True)
    return centred * lax.rsqrt(spread + 1e-05) * scale + shift


def rotary_tables(length, dims):
    half = dims // 2
    position = jnp.arange(length).astype(jnp.float32)
    rates = 10000.0 ** (-(2.0 * jnp.arange(half).astype(jnp.float32)) / dims)
    angles = position[:, None] * rates[None, :]
    return (jnp.cos(angles), jnp.sin(angles))


def rotate(values, cosine, sine):
    half = cosine.shape[-1]
    cosine = cosine[None, :, None, :]
    sine = sine[None, :, None, :]
    first = values[..., :half]
    second = values[..., half : 2 * half]
    return jnp.concatenate(
        [first * cosine - second * sine, second * cosine + first * sine, values[..., 2 * half :]],
        axis=-1,
    )


def contract_rows(left, right):
    return lax.dot_general(
        left, right, (((0,), (0,)), ((), ())), preferred_element_type=jnp.float32
    )


def contract_cols(left, right):
    return lax.dot_general(
        left, right, (((1,), (1,)), ((), ())), preferred_element_type=jnp.float32
    )


def local_forward(rows16, params, cosine, sine, causal):
    (
        heads_full,
        heads_offset,
        merge_full,
        merge_offset,
        up_full,
        up_offset,
        down_full,
        down_offset,
        first_scale,
        first_move,
        second_scale,
        second_move,
    ) = params
    inputs = rows16.astype(jnp.float32)
    count = rows16.shape[0] // SEQ
    local_heads = heads_full.shape[1] // (3 * HD)
    scaling = 1.0 / math.sqrt(HD)
    first_normed = layer_norm(
        inputs, first_scale.astype(jnp.float32), first_move.astype(jnp.float32)
    ).astype(jnp.bfloat16)
    second_normed = layer_norm(
        inputs, second_scale.astype(jnp.float32), second_move.astype(jnp.float32)
    ).astype(jnp.bfloat16)
    mixed = jnp.dot(
        first_normed, heads_full, preferred_element_type=jnp.float32
    ) + heads_offset.astype(jnp.float32)
    mixed = mixed.reshape(count, SEQ, local_heads, 3, HD)
    query = rotate(mixed[:, :, :, 0], cosine, sine).astype(jnp.bfloat16)
    keys = rotate(mixed[:, :, :, 1], cosine, sine).astype(jnp.bfloat16)
    values = mixed[:, :, :, 2].astype(jnp.bfloat16)
    scores = (
        jnp.einsum("csha,ctha->chst", query, keys, preferred_element_type=jnp.float32) * scaling
    )
    probs = jax.nn.softmax(jnp.where(causal, scores, -1e30), axis=-1)
    weights16 = probs.astype(jnp.bfloat16)
    attended = jnp.einsum("chst,ctha->csha", weights16, values, preferred_element_type=jnp.float32)
    attended = attended.reshape(rows16.shape[0], local_heads * HD).astype(jnp.bfloat16)
    hidden = jnp.dot(second_normed, up_full, preferred_element_type=jnp.float32) + up_offset.astype(
        jnp.float32
    )
    activated = jax.nn.gelu(hidden, approximate=False).astype(jnp.bfloat16)
    branches = jnp.dot(attended, merge_full, preferred_element_type=jnp.float32)
    branches = branches + jnp.dot(activated, down_full, preferred_element_type=jnp.float32)
    saved = (
        inputs,
        first_normed,
        second_normed,
        query,
        keys,
        values,
        probs,
        weights16,
        attended,
        hidden,
        activated,
    )
    return (branches, saved)


def local_backward(grad16, saved, params, cosine, sine):
    (
        heads_full,
        heads_offset,
        merge_full,
        merge_offset,
        up_full,
        up_offset,
        down_full,
        down_offset,
        first_scale,
        first_move,
        second_scale,
        second_move,
    ) = params
    (
        inputs,
        first_normed,
        second_normed,
        query,
        keys,
        values,
        probs,
        weights16,
        attended,
        hidden,
        activated,
    ) = saved
    rows = grad16.shape[0]
    count = rows // SEQ
    local_heads = heads_full.shape[1] // (3 * HD)
    scaling = 1.0 / math.sqrt(HD)
    grad32 = grad16.astype(jnp.float32)
    merge_grad = contract_rows(attended, grad16)
    down_grad = contract_rows(activated, grad16)
    bias_grad = jnp.sum(grad32, axis=0)
    d_attended = (
        contract_cols(grad16, merge_full).astype(jnp.bfloat16).reshape(count, SEQ, local_heads, HD)
    )
    d_activated = contract_cols(grad16, down_full)
    gelu_value, gelu_pull = jax.vjp(partial(jax.nn.gelu, approximate=False), hidden)
    d_hidden = gelu_pull(d_activated)[0].astype(jnp.bfloat16)
    up_grad = contract_rows(second_normed, d_hidden)
    up_bias_grad = jnp.sum(d_hidden.astype(jnp.float32), axis=0)
    d_values = jnp.einsum(
        "chst,csha->ctha", weights16, d_attended, preferred_element_type=jnp.float32
    )
    d_probs = jnp.einsum("csha,ctha->chst", d_attended, values, preferred_element_type=jnp.float32)
    d_scores = probs * (d_probs - jnp.sum(d_probs * probs, axis=-1, keepdims=True))
    d_scores = (d_scores * scaling).astype(jnp.bfloat16)
    d_query = jnp.einsum("chst,ctha->csha", d_scores, keys, preferred_element_type=jnp.float32)
    d_keys = jnp.einsum("chst,csha->ctha", d_scores, query, preferred_element_type=jnp.float32)
    d_mixed = jnp.stack(
        [rotate(d_query, cosine, -sine), rotate(d_keys, cosine, -sine), d_values], axis=3
    )
    d_mixed = d_mixed.reshape(rows, local_heads * 3 * HD).astype(jnp.bfloat16)
    heads_grad = contract_rows(first_normed, d_mixed)
    heads_bias_grad = jnp.sum(d_mixed.astype(jnp.float32), axis=0)
    d_first = contract_cols(d_mixed, heads_full)
    d_second = contract_cols(d_hidden, up_full)
    first_value, first_pull = jax.vjp(
        layer_norm, inputs, first_scale.astype(jnp.float32), first_move.astype(jnp.float32)
    )
    first_input, first_gain_grad, first_shift_grad = first_pull(d_first)
    second_value, second_pull = jax.vjp(
        layer_norm, inputs, second_scale.astype(jnp.float32), second_move.astype(jnp.float32)
    )
    second_input, second_gain_grad, second_shift_grad = second_pull(d_second)
    grads = (
        heads_grad,
        heads_bias_grad,
        merge_grad,
        bias_grad,
        up_grad,
        up_bias_grad,
        down_grad,
        bias_grad,
        first_gain_grad,
        first_shift_grad,
        second_gain_grad,
        second_shift_grad,
    )
    return (first_input + second_input, grads)


def body(
    block_input,
    cotangent,
    heads_weight,
    heads_bias,
    merge_weight,
    merge_bias,
    up_weight,
    up_bias,
    down_weight,
    down_bias,
    first_gain,
    first_shift,
    second_gain,
    second_shift,
):
    rows_batch = block_input.shape[0] // MB
    cosine, sine = rotary_tables(SEQ, ROT)
    causal = jnp.arange(SEQ)[:, None] >= jnp.arange(SEQ)[None, :]
    totals = None
    outputs = []
    input_grads = []
    for batch in range(MB):
        rows16 = block_input[batch * rows_batch : (batch + 1) * rows_batch]
        grad16 = cotangent[batch * rows_batch : (batch + 1) * rows_batch]
        forward_set = (
            lax.all_gather(heads_weight, "dp", axis=0, tiled=True),
            lax.all_gather(heads_bias, "dp", axis=0, tiled=True),
            lax.all_gather(merge_weight, "dp", axis=1, tiled=True),
            lax.all_gather(merge_bias, "dp", axis=0, tiled=True),
            lax.all_gather(up_weight, "dp", axis=0, tiled=True),
            lax.all_gather(up_bias, "dp", axis=0, tiled=True),
            lax.all_gather(down_weight, "dp", axis=1, tiled=True),
            lax.all_gather(down_bias, "dp", axis=0, tiled=True),
            lax.all_gather(first_gain, "dp", axis=0, tiled=True),
            lax.all_gather(first_shift, "dp", axis=0, tiled=True),
            lax.all_gather(second_gain, "dp", axis=0, tiled=True),
            lax.all_gather(second_shift, "dp", axis=0, tiled=True),
        )
        branches, saved = local_forward(rows16, forward_set, cosine, sine, causal)
        biases = forward_set[3].astype(jnp.float32) + forward_set[7].astype(jnp.float32)
        summed = lax.psum(branches.astype(jnp.bfloat16), "tensor").astype(jnp.float32)
        outputs.append((saved[0] + summed + biases).astype(jnp.bfloat16))
        backward_set = (
            lax.all_gather(heads_weight, "dp", axis=0, tiled=True),
            lax.all_gather(heads_bias, "dp", axis=0, tiled=True),
            lax.all_gather(merge_weight, "dp", axis=1, tiled=True),
            lax.all_gather(merge_bias, "dp", axis=0, tiled=True),
            lax.all_gather(up_weight, "dp", axis=0, tiled=True),
            lax.all_gather(up_bias, "dp", axis=0, tiled=True),
            lax.all_gather(down_weight, "dp", axis=1, tiled=True),
            lax.all_gather(down_bias, "dp", axis=0, tiled=True),
            lax.all_gather(first_gain, "dp", axis=0, tiled=True),
            lax.all_gather(first_shift, "dp", axis=0, tiled=True),
            lax.all_gather(second_gain, "dp", axis=0, tiled=True),
            lax.all_gather(second_shift, "dp", axis=0, tiled=True),
        )
        partial_input, grads = local_backward(grad16, saved, backward_set, cosine, sine)
        reduced = (
            lax.psum(partial_input.astype(jnp.bfloat16), "tensor").astype(jnp.float32),
            lax.psum(grads[8].astype(jnp.bfloat16), "tensor").astype(jnp.float32),
            lax.psum(grads[9].astype(jnp.bfloat16), "tensor").astype(jnp.float32),
            lax.psum(grads[10].astype(jnp.bfloat16), "tensor").astype(jnp.float32),
            lax.psum(grads[11].astype(jnp.bfloat16), "tensor").astype(jnp.float32),
        )
        input_grads.append(reduced[0] + grad16.astype(jnp.float32))
        grads = grads[:8] + (reduced[1], reduced[2], reduced[3], reduced[4])
        if totals is None:
            totals = grads
        else:
            totals = tuple((old + new for old, new in zip(totals, grads)))
    scattered = (
        lax.psum_scatter(totals[0], "dp", scatter_dimension=0, tiled=True),
        lax.psum_scatter(totals[1], "dp", scatter_dimension=0, tiled=True),
        lax.psum_scatter(totals[2], "dp", scatter_dimension=1, tiled=True),
        lax.psum_scatter(totals[3], "dp", scatter_dimension=0, tiled=True),
        lax.psum_scatter(totals[4], "dp", scatter_dimension=0, tiled=True),
        lax.psum_scatter(totals[5], "dp", scatter_dimension=0, tiled=True),
        lax.psum_scatter(totals[6], "dp", scatter_dimension=1, tiled=True),
        lax.psum_scatter(totals[7], "dp", scatter_dimension=0, tiled=True),
        lax.psum_scatter(totals[8], "dp", scatter_dimension=0, tiled=True),
        lax.psum_scatter(totals[9], "dp", scatter_dimension=0, tiled=True),
        lax.psum_scatter(totals[10], "dp", scatter_dimension=0, tiled=True),
        lax.psum_scatter(totals[11], "dp", scatter_dimension=0, tiled=True),
    )
    layer_output = jnp.concatenate(outputs, axis=0)
    input_grad = jnp.concatenate(input_grads, axis=0)
    return (
        layer_output,
        input_grad,
        scattered[0],
        scattered[1],
        scattered[2],
        scattered[3],
        scattered[4],
        scattered[5],
        scattered[6],
        scattered[7],
        scattered[8],
        scattered[9],
        scattered[10],
        scattered[11],
    )


def solution(mesh):
    placed = (
        P("dp", None),
        P("dp", None),
        P("dp", "tensor"),
        P(("tensor", "dp")),
        P("tensor", "dp"),
        P("dp"),
        P("dp", "tensor"),
        P(("tensor", "dp")),
        P("tensor", "dp"),
        P("dp"),
        P("dp"),
        P("dp"),
        P("dp"),
        P("dp"),
    )
    return jax.shard_map(
        body,
        mesh=mesh,
        in_specs=placed,
        out_specs=(
            P("dp", None),
            P("dp", None),
            P("dp", "tensor"),
            P(("tensor", "dp")),
            P("tensor", "dp"),
            P("dp"),
            P("dp", "tensor"),
            P(("tensor", "dp")),
            P("tensor", "dp"),
            P("dp"),
            P("dp"),
            P("dp"),
            P("dp"),
            P("dp"),
        ),
        check_vma=False,
    )
```

profile of v0, /device:TPU:0, one launch (start us, length us, event | category | flops | bytes accessed | tf_op | source)
XLA Modules:
  0.0 784.7 jit_solution(5532399431525647224)
XLA Ops:
  10.5 11.0 %all_gather.28 = bf16[192,768]{0,1:T(8,128)(2,1)S(1)} all-gather(bf16[192,96]{0,1:T(8,128)(2,1)S(1)} %copy.96), channel_id=1, replica_groups=mesh['dp'=8,'tensor'=4] {'dp'}, dimensions={1}, use_global_device_ids=true | all-gather | bytes 331776 | tf_op jit(solution)/shard_map/all_gather | solution.py:228
  21.6 3.6 convolution_convert_fusion
  25.1 3.5 convolution_convert_fusion.1
  32.4 24.2 %all-reduce.16 = (bf16[768]{0:T(1024)(128)(2,1)}, bf16[768]{0:T(1024)(128)(2,1)S(1)}, bf16[768]{0:T(1024)(128)(2,1)S(1)}, bf16[576]{0:T(1024)(128)(2,1)S(1)}, bf...) all-reduce(bf16[768]{0:T(1024)(128)(2,1)S(1)} %dynamic-update-slice, ...), channel_id=1, replica_groups=mesh['dp'=8,'tensor'=4] {'dp'}, use_global_device_ids=true, to_apply=%add.4 | all-reduce | flops 5952 | bytes 23808
  56.7 2.2 convert_reduce_fusion
  58.9 3.2 convert_reduce_fusion.1
  62.1 10.8 %all_gather.26 = bf16[768,576]{1,0:T(8,128)(2,1)S(1)} all-gather(bf16[96,576]{1,0:T(8,128)(2,1)S(1)} %copy-done.29), channel_id=1, replica_groups=mesh['dp'=8,'tensor'=4] {'dp'}, dimensions={0}, use_global_device_ids=true | all-gather | bytes 995328 | tf_op jit(solution)/shard_map/all_gather | solution.py:226
  73.9 4.0 convolution_add_fusion
  78.0 6.6 reshape.250
  84.6 2.6 slice.151
  87.2 2.5 fusion.192
  89.7 2.1 reshape.252
  93.2 5.1 fusion.149
  98.3 5.6 fusion.194
  104.0 5.4 fusion.99
  111.6 13.8 %fusion.102 = f32[3,512,3,64]{1,3,2,0:T(8,128)S(1)} fusion(f32[3,3,512,512]{2,3,1,0:T(8,128)} %fusion.149, bf16[3,512,3,48]{1,3,2,0:T(8,128)(2,1)S(1)} %copy-done.21, bf16[3,512,3,8]{1,3,2,0:T(8,128)(2,1)S(1)} %copy-done.49, bf16[3,512,3,8]{1,3,2,0:T(8,128)(2,1)S(1)} %copy-done.51, f32[3,3,512,512]{2,3,1,0:T(8,128)} %get-tuple-element.122, ...), kind=kOutput, calls=%fused_computation.151 | convolution fusion | flops 320279552 | bytes 20662272 | tf_op jit(solution)/shard_map/chst,ctha->csha/dot_general | solution.py:165
  125.4 14.7 %fusion.105 = f32[3,512,3,64]{1,3,2,0:T(8,128)} fusion(f32[3,3,512,512]{2,3,1,0:T(8,128)} %fusion.149, bf16[3,512,3,48]{1,3,2,0:T(8,128)(2,1)S(1)} %slice.279, bf16[3,512,3,8]{1,3,2,0:T(8,128)(2,1)} %copy-done.43, bf16[3,512,3,8]{1,3,2,0:T(8,128)(2,1)S(1)} %get-tuple-element.99, f32[3,3,512,512]{2,3,1,0:T(8,128)} %get-tuple-element.122, ...), kind=kOutput, calls=%fused_computation.152 | convolution fusion | flops 320279552 | bytes 20662272 | tf_op jit(solution)/shard_map/chst,csha->ctha/dot_general | solution.py:166
  140.2 1.6 reshape.251
  146.7 1.5 copy.113
  148.9 15.8 %multiply_convert_fusion.2 = (bf16[1536,768]{1,0:T(8,128)(2,1)}, f32[1536,768]{1,0:T(8,128)}, f32[1536,768]{1,0:T(8,128)}) fusion(f32[768]{0:T(1024)S(1)} %convert_element_type.381, bf16[768,768]{1,0:T(8,128)(2,1)} %all-gather.3.cloned.1.call-done, f32[1536]{0:T(1024)S(1)} %fusion.159, f32[1536]{0:T(1024)S(1)} %broadcast_multiply_fusion, ...), kind=kOutput, calls=%fused_computation.89 | convolution fusion | flops 1896873984 | bytes 15356928 | tf_op jit(solution)/shard_map/dot_general | solution.py:93
  164.8 8.8 %convert_reduce_fusion.4 = (f32[768]{0:T(1024)}, bf16[1536,768]{1,0:T(8,128)(2,1)S(1)}) fusion(f32[1536,768]{1,0:T(8,128)} %get-tuple-element.77, bf16[768,768]{0,1:T(8,128)(2,1)} %all-gather.5.cloned.1.call-done, bf16[3072,768]{1,0:T(8,128)(2,1)} %param.15, f32[1536,768]{1,0:T(8,128)} %get-tuple-element.120, f32[768]{0:T(1024)S(1)} %convert_element_type.381), kind=kOutput, calls=%fused_computation.82 | convolution fusion | flops 1831992576 | bytes 15341568 | tf_op jit(solution)/shard_map/dot_general | solution.py:49
  173.6 2.0 fusion.199
  175.8 9.9 %fusion.63 = (f32[1536]{0:T(1024)}, f32[1536]{0:T(1024)}, bf16[768]{0:T(1024)(128)(2,1)}, f32[1536]{0:T(1024)S(1)}, f32[1536,768]{1,0:T(8,128)}) fusion(f32[1536]{0:T(1024)S(1)} %broadcast_multiply_fusion, f32[768]{0:T(1024)S(1)} %convert_element_type.367, bf16[3072,768]{1,0:T(8,128)(2,1)} %param.14, f32[1536,768]{1,0:T(8,128)S(1)} %fusion.199, ...), kind=kOutput, calls=%fused_computation.76 | convolution fusion | flops 1374284544 | bytes 16848384 | tf_op jit(solution)/shard_map/dot_general | solution.py:49
  186.9 2.8 convolution_add_fusion.1
  189.7 4.4 reshape.249
  194.1 1.7 slice.142
  195.8 2.4 fusion.191
  199.3 5.8 fusion.195
  205.2 5.4 fusion.96
  212.4 5.1 fusion.152
  217.5 14.7 %fusion.108 = f32[3,512,3,64]{1,3,2,0:T(8,128)} fusion(f32[3,3,512,512]{2,3,1,0:T(8,128)} %fusion.152, bf16[3,512,3,48]{1,3,2,0:T(8,128)(2,1)} %copy-done.22, bf16[3,512,3,8]{1,3,2,0:T(8,128)(2,1)S(1)} %copy-done.45, bf16[3,512,3,8]{1,3,2,0:T(8,128)(2,1)S(1)} %copy-done.47, f32[3,3,512,512]{2,3,1,0:T(8,128)} %get-tuple-element.126, ...), kind=kOutput, calls=%fused_computation.153 | convolution fusion | flops 320279552 | bytes 20662272 | tf_op jit(solution)/shard_map/chst,ctha->csha/dot_general | solution.py:165
  232.3 15.1 %fusion.111 = f32[3,512,3,64]{1,3,2,0:T(8,128)} fusion(f32[3,3,512,512]{2,3,1,0:T(8,128)} %fusion.152, bf16[3,512,3,48]{1,3,2,0:T(8,128)(2,1)S(1)} %slice.281, bf16[3,512,3,8]{1,3,2,0:T(8,128)(2,1)S(1)} %copy-done.42, bf16[3,512,3,8]{1,3,2,0:T(8,128)(2,1)S(1)} %copy-done.40, f32[3,3,512,512]{2,3,1,0:T(8,128)} %get-tuple-element.126, ...), kind=kOutput, calls=%fused_computation.154 | convolution fusion | flops 320279552 | bytes 20662272 | tf_op jit(solution)/shard_map/chst,csha->ctha/dot_general | solution.py:166
  247.4 1.4 slice.165
  252.0 2.6 fusion.139
  254.6 2.0 fusion.197
  256.7 2.3 add_convert_fusion.4
  262.0 1.5 copy.107
  263.5 1.8 copy.133
  265.5 13.8 %multiply_convert_fusion.3 = (bf16[1536,768]{1,0:T(8,128)(2,1)}, f32[1536,768]{1,0:T(8,128)S(1)}, f32[1536,768]{1,0:T(8,128)S(1)}) fusion(f32[768]{0:T(1024)S(1)} %copy-done.80, bf16[768,768]{1,0:T(8,128)(2,1)S(1)} %copy-done.96, f32[768]{0:T(1024)S(1)} %copy-done.77, f32[768]{0:T(1024)S(1)} %copy-done.56, f32[1536]{0:T(1024)S(1)} %copy-done.35, ...), kind=kOutput, calls=%fused_computation.104 | convolution fusion | flops 1896873984 | bytes 15364096 | tf_op jit(solution)/shard_map/dot_general | solution.py:93
  279.3 4.1 convert_reduce_fusion.5
  283.4 2.1 fusion.198
  285.6 10.0 %fusion.57 = (f32[1536]{0:T(1024)S(1)}, f32[1536]{0:T(1024)S(1)}, bf16[768]{0:T(1024)(128)(2,1)}, f32[1536]{0:T(1024)S(1)}, f32[1536]{0:T(1024)S(1)}, /*index=5*...) fusion(f32[768]{0:T(1024)S(1)} %copy-done.53, ...), kind=kOutput, calls=%fused_computation.70 | convolution fusion | flops 1393155072 | bytes 26314752 | tf_op jit(solution)/shard_map/dot_general | solution.py:49
  295.6 9.0 %fusion.55 = (bf16[768]{0:T(1024)(128)(2,1)}, f32[1536]{0:T(1024)S(1)}, f32[1536]{0:T(1024)S(1)}, bf16[768]{0:T(1024)(128)(2,1)}, bf16[768]{0:T(1024)(128)(2,1)}, /*index=5*/bf16[1536,768]{1,0:T(8,128)(2,1)}) fusion(f32[1536,768]{1,0:T(8,128)S(1)} %fusion.198, f32[1536]{0:T(1024)S(1)} %copy-done.35, f32[1536]{0:T(1024)S(1)} %copy-done.33, ...), kind=kLoop, calls=%fused_computation.68 | loop fusion | flops 42461952 | bytes 26036736 | tf_op jit(solution)/shard_map/transpose(jvp())/reduce_sum | solution.py:19
  304.7 2.0 fusion.196
  306.7 2.3 add_convert_fusion.5
  309.0 3.8 add_convert_fusion.2
  312.9 1.4 copy-done.16
  314.3 4.2 fusion.178
  318.6 6.0 convolution_add_fusion.4
  325.0 5.0 fusion.181
  330.0 5.7 convolution_add_fusion.3
  337.1 4.6 fusion.137
  341.9 5.3 convolution_add_fusion.2
  347.5 23.0 %all-reduce.17 = (bf16[768]{0:T(1024)(128)(2,1)S(1)}, bf16[768]{0:T(1024)(128)(2,1)S(1)}, bf16[768]{0:T(1024)(128)(2,1)S(1)}, bf16[768]{0:T(1024)(128)(2,1)S(1)}...) all-reduce(bf16[768]{0:T(1024)(128)(2,1)S(1)} %copy-done.88, ...), channel_id=1, replica_groups=mesh['dp'=8,'tensor'=4] {'tensor'}, use_global_device_ids=true, to_apply=%region_38.39 | all-reduce | flops 6144 | bytes 24576 | tf_op jit(solution)/shard_map/psum | solution.py:260
  370.5 1.6 copy.124
  372.2 268.4 %all-reduce.21.cloned.1.call-done = (bf16[1536,768]{1,0:T(8,128)(2,1)}, bf16[1536,768]{1,0:T(8,128)(2,1)}, bf16[1536,768]{1,0:T(8,128)(2,1)}, bf16[1536,768]{1,0:T(8,128)(2,1)}) async-done(((bf16[1536,768]{1,0:T(8,128)(2,1)}, bf16[1536,768]{1,0:T(8,128)(2,1)}, bf16[1536,768]{1,0:T(8,128)(2,1)}, bf16[1536,768]{1,0:T(8,128)(2,1)}), (bf16[1536,768]{1,0:T(8,128)(2,1)}, bf16[1536,768]{1,0:T(8,128)(2,1)}, ...) | async-done | bytes 9437200 | tf_op jit(solution)/shard_map/psum | solution.py:241
  640.6 6.8 convert_reduce_fusion.2
  647.4 24.8 %all-reduce.15 = (f32[576]{0:T(1024)S(1)}, f32[768]{0:T(1024)S(1)}, f32[768]{0:T(1024)S(1)}, f32[768]{0:T(1024)S(1)}, f32[768]{0:T(1024)S(1)}, /*index=5*/f32[768]{0:T(1024)S(1)}, f32[768]{0:T(1024)S(1)}) all-reduce(f32[576]{0:T(1024)S(1)} %add.272, f32[768]{0:T(1024)S(1)} %add.274, ...), channel_id=3, replica_groups=mesh['dp'=8,'tensor'=4] {'dp'}, use_global_device_ids=true, to_apply=%region_25.26.clone | all-reduce | flops 5184 | bytes 41472
  675.8 4.0 fusion.60
  679.8 2.7 pad_maximum_fusion.1
  683.8 1.5 copy-done.1
  685.3 4.3 pad_maximum_fusion
  689.7 40.7 %reduce-scatter.9.cloned.1.call-done = f32[96,768]{1,0:T(8,128)} async-done(((f32[768,768]{1,0:T(8,128)}), f32[96,768]{1,0:T(8,128)}) %reduce-scatter.9.cloned.1.call-update) | async-done | bytes 294928 | tf_op jit(solution)/shard_map/reduce_scatter | solution.py:276
  730.4 46.4 %reduce-scatter.11.cloned.1.call-done = f32[768,96]{0,1:T(8,128)} async-done(((f32[768,768]{0,1:T(8,128)}), f32[768,96]{0,1:T(8,128)}) %reduce-scatter.11.cloned.1.call-update) | async-done | bytes 294928 | tf_op jit(solution)/shard_map/reduce_scatter | solution.py:278
  (366 shorter events, 32.2 us)
Async XLA Ops:
  7.2 21.5 %copy-start.84 = (u32[32]{0:T(128)S(1)}, u32[32]{0:T(128)}, u32[]{:S(2)}) copy-start(u32[32]{0:T(128)} %constant.97) | copy-start | bytes 388
  7.2 23.4 %copy-start.97 = (bf16[96]{0:T(256)(128)(2,1)S(1)}, bf16[96]{0:T(256)(128)(2,1)}, u32[]{:S(2)}) copy-start(bf16[96]{0:T(256)(128)(2,1)} %param.23) | copy-start | bytes 580
  7.2 23.6 %copy-start.98 = (bf16[96]{0:T(256)(128)(2,1)S(1)}, bf16[96]{0:T(256)(128)(2,1)}, u32[]{:S(2)}) copy-start(bf16[96]{0:T(256)(128)(2,1)} %param.24) | copy-start | bytes 580
  7.2 23.8 %copy-start.99 = (bf16[96]{0:T(256)(128)(2,1)S(1)}, bf16[96]{0:T(256)(128)(2,1)}, u32[]{:S(2)}) copy-start(bf16[96]{0:T(256)(128)(2,1)} %param.25) | copy-start | bytes 580
  7.2 24.1 %copy-start.100 = (bf16[96]{0:T(256)(128)(2,1)S(1)}, bf16[96]{0:T(256)(128)(2,1)}, u32[]{:S(2)}) copy-start(bf16[96]{0:T(256)(128)(2,1)} %param.21) | copy-start | bytes 580
  7.2 24.3 %copy-start.101 = (bf16[96]{0:T(256)(128)(2,1)S(1)}, bf16[96]{0:T(256)(128)(2,1)}, u32[]{:S(2)}) copy-start(bf16[96]{0:T(256)(128)(2,1)} %param.26) | copy-start | bytes 580
  7.2 24.5 %copy-start.102 = (bf16[96]{0:T(256)(128)(2,1)S(1)}, bf16[96]{0:T(256)(128)(2,1)}, u32[]{:S(2)}) copy-start(bf16[96]{0:T(256)(128)(2,1)} %param.27) | copy-start | bytes 580
  7.3 24.7 %copy-start.103 = (bf16[96]{0:T(256)(128)(2,1)S(1)}, bf16[96]{0:T(256)(128)(2,1)}, u32[]{:S(2)}) copy-start(bf16[96]{0:T(256)(128)(2,1)} %param.19) | copy-start | bytes 580
  7.3 25.0 %copy-start.104 = (bf16[72]{0:T(256)(128)(2,1)S(1)}, bf16[72]{0:T(256)(128)(2,1)}, u32[]{:S(2)}) copy-start(bf16[72]{0:T(256)(128)(2,1)} %param.17) | copy-start | bytes 436
  7.3 141.6 %all-gather.3.cloned.1.call-start = ((), (), s32[]{:S(2)}) async-start(), calls=%async_computation.4 | async-start | bytes 1327104 | tf_op jit(solution)/shard_map/all_gather | solution.py:230
  8.0 156.8 %all-gather.5.cloned.1.call-start = ((), (), s32[]{:S(2)}) async-start(), calls=%async_computation.5 | async-start | bytes 1327104 | tf_op jit(solution)/shard_map/all_gather | solution.py:232
  8.8 361.8 %reduce-scatter.13.cloned.1.call-start = ((), (), s32[]{:S(2)}) async-start(), calls=%async_computation.9 | async-start | bytes 884736
  25.1 36.9 %copy-start.29 = (bf16[96,576]{1,0:T(8,128)(2,1)S(1)}, bf16[96,576]{1,0:T(8,128)(2,1)}, u32[]{:S(2)}) copy-start(bf16[96,576]{1,0:T(8,128)(2,1)} %param.16) | copy-start | bytes 331780
  25.1 48.8 %slice-start = ((s8[4718592]{0:T(1024)(128)(4,1)}), s8[524288]{0:T(1024)(128)(4,1)S(1)}, s32[]{:S(2)}) async-start(s8[4718592]{0:T(1024)(128)(4,1)} %bitcast.111), calls=%async_computation.11 | async-start | bytes 1048576
  56.6 119.1 %copy-start.52 = (f32[768]{0:T(1024)}, f32[768]{0:T(1024)S(1)}, u32[]{:S(2)}) copy-start(f32[768]{0:T(1024)S(1)} %convert_element_type.367) | copy-start | bytes 9220
  56.6 21.4 %copy-start.73 = (f32[768]{0:T(1024)}, f32[768]{0:T(1024)S(1)}, u32[]{:S(2)}) copy-start(f32[768]{0:T(1024)S(1)} %convert_element_type.368) | copy-start | bytes 9220
  56.6 21.3 %copy-start.81 = (f32[576]{0:T(1024)}, f32[576]{0:T(1024)S(1)}, u32[]{:S(2)}) copy-start(f32[576]{0:T(1024)S(1)} %convert_element_type.370) | copy-start | bytes 6916
  56.7 17.3 %slice-start.1 = ((s8[4718592]{0:T(1024)(128)(4,1)}), s8[4194304]{0:T(1024)(128)(4,1)S(1)}, s32[]{:S(2)}) async-start(s8[4718592]{0:T(1024)(128)(4,1)} %bitcast.111), calls=%async_computation.12 | async-start | bytes 8388608
  58.9 116.8 %copy-start.30 = (f32[1536]{0:T(1024)}, f32[1536]{0:T(1024)S(1)}, u32[]{:S(2)}) copy-start(f32[1536]{0:T(1024)S(1)} %broadcast_multiply_fusion) | copy-start | bytes 18436
  62.1 15.9 %copy-start.37 = (f32[1536]{0:T(1024)}, f32[1536]{0:T(1024)S(1)}, u32[]{:S(2)}) copy-start(f32[1536]{0:T(1024)S(1)} %get-tuple-element.42) | copy-start | bytes 18436
  62.1 86.8 %copy-start.58 = (f32[1536]{0:T(1024)}, f32[1536]{0:T(1024)S(1)}, u32[]{:S(2)}) copy-start(f32[1536]{0:T(1024)S(1)} %fusion.159) | copy-start | bytes 18436
  92.8 51.8 %copy-start.25 = (f32[512,8]{0,1:T(8,128)}, f32[512,8]{0,1:T(8,128)S(1)}, u32[]{:S(2)}) copy-start(f32[512,8]{0,1:T(8,128)S(1)} %get-tuple-element.115) | copy-start | bytes 49156
  104.0 6.6 copy-start.109
  125.4 14.8 %copy-start.83 = (bf16[768]{0:T(1024)(128)(2,1)S(1)}, bf16[768]{0:T(1024)(128)(2,1)}, u32[]{:S(2)}) copy-start(bf16[768]{0:T(1024)(128)(2,1)} %get-tuple-element.50) | copy-start | bytes 4612
  125.4 14.8 %copy-start.19 = (bf16[1536,192]{0,1:T(8,128)(2,1)S(1)}, bf16[1536,192]{0,1:T(8,128)(2,1)}, u32[]{:S(2)}) copy-start(bf16[1536,192]{0,1:T(8,128)(2,1)} %convolution_convert_fusion.1) | copy-start | bytes 1769476
  140.2 8.7 %copy-start.76 = (f32[768]{0:T(1024)}, f32[768]{0:T(1024)S(1)}, u32[]{:S(2)}) copy-start(f32[768]{0:T(1024)S(1)} %convert_element_type.379) | copy-start | bytes 9220
  140.2 35.5 %copy-start.55 = (f32[768]{0:T(1024)}, f32[768]{0:T(1024)S(1)}, u32[]{:S(2)}) copy-start(f32[768]{0:T(1024)S(1)} %convert_element_type.378) | copy-start | bytes 9220
  140.2 24.6 %copy-start.79 = (f32[768]{0:T(1024)}, f32[768]{0:T(1024)S(1)}, u32[]{:S(2)}) copy-start(f32[768]{0:T(1024)S(1)} %convert_element_type.381) | copy-start | bytes 9220
  140.2 35.5 %copy-start.32 = (f32[1536]{0:T(1024)}, f32[1536]{0:T(1024)S(1)}, u32[]{:S(2)}) copy-start(f32[1536]{0:T(1024)S(1)} %broadcast_multiply_fusion.1) | copy-start | bytes 18436
  148.8 26.9 %copy-start.14 = (bf16[72,8,3,512]{3,1,2,0:T(8,128)(2,1)}, bf16[72,8,3,512]{3,1,2,0:T(8,128)(2,1)S(1)}, u32[]{:S(2)}) copy-start(bf16[72,8,3,512]{3,1,2,0:T(8,128)(2,1)S(1)} %copy.134) | copy-start | bytes 5308420
  164.8 8.8 %copy-start.95 = (bf16[768,768]{1,0:T(8,128)(2,1)S(1)}, bf16[768,768]{1,0:T(8,128)(2,1)}, u32[]{:S(2)}) copy-start(bf16[768,768]{1,0:T(8,128)(2,1)} %all-gather.3.cloned.1.call-done) | copy-start | bytes 3538948
  173.6 13.3 %slice-start.2 = ((s8[4718592]{0:T(1024)(128)(4,1)}), s8[4194304]{0:T(1024)(128)(4,1)S(1)}, s32[]{:S(2)}) async-start(s8[4718592]{0:T(1024)(128)(4,1)} %bitcast.113), calls=%async_computation.13 | async-start | bytes 8388608
  175.7 10.0 %copy-start.2 = (f32[1536,768]{1,0:T(8,128)}, f32[1536,768]{1,0:T(8,128)S(1)}, u32[]{:S(2)}) copy-start(f32[1536,768]{1,0:T(8,128)S(1)} %fusion.199) | copy-start | bytes 14155780
  175.8 11.2 %slice-start.3 = ((s8[4718592]{0:T(1024)(128)(4,1)}), s8[524288]{0:T(1024)(128)(4,1)S(1)}, s32[]{:S(2)}) async-start(s8[4718592]{0:T(1024)(128)(4,1)} %bitcast.113), calls=%async_computation.14 | async-start | bytes 1048576
  175.8 11.1 %copy-start.74 = (f32[768]{0:T(1024)S(1)}, f32[768]{0:T(1024)}, u32[]{:S(2)}) copy-start(f32[768]{0:T(1024)} %copy-done.73) | copy-start | bytes 9220
  175.8 11.1 %copy-start.82 = (f32[576]{0:T(1024)S(1)}, f32[576]{0:T(1024)}, u32[]{:S(2)}) copy-start(f32[576]{0:T(1024)} %copy-done.81) | copy-start | bytes 6916
  199.2 5.9 copy-start.39
  199.2 5.9 copy-start.41
  205.2 6.4 copy-start.108
  217.5 14.7 %copy-start.40 = (bf16[3,512,3,8]{1,3,2,0:T(8,128)(2,1)S(1)}, bf16[3,512,3,8]{1,3,2,0:T(8,128)(2,1)}, u32[]{:S(2)}) copy-start(bf16[3,512,3,8]{1,3,2,0:T(8,128)(2,1)} %copy-done.39) | copy-start | bytes 221188
  217.5 14.7 %copy-start.42 = (bf16[3,512,3,8]{1,3,2,0:T(8,128)(2,1)S(1)}, bf16[3,512,3,8]{1,3,2,0:T(8,128)(2,1)}, u32[]{:S(2)}) copy-start(bf16[3,512,3,8]{1,3,2,0:T(8,128)(2,1)} %copy-done.41) | copy-start | bytes 221188
  232.2 16.6 %copy-start.26 = (f32[512,8]{0,1:T(8,128)S(1)}, f32[512,8]{0,1:T(8,128)}, u32[]{:S(2)}) copy-start(f32[512,8]{0,1:T(8,128)} %copy-done.25) | copy-start | bytes 49156
  247.4 7.2 copy-start.92
  247.4 7.2 copy-start.106
  251.8 7.2 slice-start.6
  260.8 379.8 %all-reduce.21.cloned.1.call-start = ((), (), s32[]{:S(2)}) async-start(), calls=%async_computation.10 | async-start | bytes 18874368 | tf_op jit(solution)/shard_map/psum | solution.py:241
  261.9 17.3 %slice-start.8 = ((s8[4718592]{0:T(1024)(128)(4,1)}), s8[4194304]{0:T(1024)(128)(4,1)S(1)}, s32[]{:S(2)}) async-start(s8[4718592]{0:T(1024)(128)(4,1)} %bitcast.121), calls=%async_computation.19 | async-start | bytes 8388608
  261.9 23.6 %slice-start.10 = ((s8[4718592]{0:T(1024)(128)(4,1)}), s8[4194304]{0:T(1024)(128)(4,1)S(1)}, s32[]{:S(2)}) async-start(s8[4718592]{0:T(1024)(128)(4,1)} %bitcast.123), calls=%async_computation.21 | async-start | bytes 8388608
  262.0 23.6 %slice-start.12 = ((s8[4718592]{0:T(1024)(128)(4,1)}), s8[4194304]{0:T(1024)(128)(4,1)S(1)}, s32[]{:S(2)}) async-start(s8[4718592]{0:T(1024)(128)(4,1)} %bitcast.125), calls=%async_computation.23 | async-start | bytes 8388608
  265.4 13.8 %slice-start.9 = ((s8[4718592]{0:T(1024)(128)(4,1)}), s8[524288]{0:T(1024)(128)(4,1)S(1)}, s32[]{:S(2)}) async-start(s8[4718592]{0:T(1024)(128)(4,1)} %bitcast.121), calls=%async_computation.20 | async-start | bytes 1048576
  265.4 13.8 %copy-start.93 = (bf16[768,768]{0,1:T(8,128)(2,1)S(1)}, bf16[768,768]{0,1:T(8,128)(2,1)}, u32[]{:S(2)}) copy-start(bf16[768,768]{0,1:T(8,128)(2,1)} %all-gather.5.cloned.1.call-done) | copy-start | bytes 3538948
  265.5 20.1 %slice-start.11 = ((s8[4718592]{0:T(1024)(128)(4,1)}), s8[524288]{0:T(1024)(128)(4,1)S(1)}, s32[]{:S(2)}) async-start(s8[4718592]{0:T(1024)(128)(4,1)} %bitcast.123), calls=%async_computation.22 | async-start | bytes 1048576
  265.5 20.1 %slice-start.13 = ((s8[4718592]{0:T(1024)(128)(4,1)}), s8[524288]{0:T(1024)(128)(4,1)S(1)}, s32[]{:S(2)}) async-start(s8[4718592]{0:T(1024)(128)(4,1)} %bitcast.125), calls=%async_computation.24 | async-start | bytes 1048576
  285.6 10.0 %copy-start.63 = (f32[1536]{0:T(1024)S(1)}, f32[1536]{0:T(1024)}, u32[]{:S(2)}) copy-start(f32[1536]{0:T(1024)} %copy-done.62) | copy-start | bytes 18436
  295.6 9.0 %copy-start.94 = (bf16[768,768]{0,1:T(8,128)(2,1)S(1)}, bf16[768,768]{0,1:T(8,128)(2,1)}, u32[]{:S(2)}) copy-start(bf16[768,768]{0,1:T(8,128)(2,1)} %all-gather.5.cloned.1.call-done) | copy-start | bytes 3538948
  295.6 9.0 %copy-start.112 = (bf16[1536,768]{1,0:T(8,128)(2,1)S(1)}, bf16[1536,768]{1,0:T(8,128)(2,1)}, u32[]{:S(2)}) copy-start(bf16[1536,768]{1,0:T(8,128)(2,1)} %get-tuple-element.74) | copy-start | bytes 7077892
  312.8 376.8 %reduce-scatter.7.cloned.1.call-start = ((), (), s32[]{:S(2)}) async-start(), calls=%async_computation.6 | async-start | bytes 2211840 | tf_op jit(solution)/shard_map/reduce_scatter | solution.py:272
  318.6 6.4 copy-start.36
  318.6 6.4 copy-start.57
  318.6 6.4 copy-start.78
  324.6 405.7 %reduce-scatter.9.cloned.1.call-start = ((), (), s32[]{:S(2)}) async-start(), calls=%async_computation.7 | async-start | bytes 2654208 | tf_op jit(solution)/shard_map/reduce_scatter | solution.py:276
  335.7 441.1 %reduce-scatter.11.cloned.1.call-start = ((), (), s32[]{:S(2)}) async-start(), calls=%async_computation.8 | async-start | bytes 2654208 | tf_op jit(solution)/shard_map/reduce_scatter | solution.py:278
  640.6 35.2 %copy-start.10 = (bf16[1536,768]{1,0:T(8,128)(2,1)S(1)}, bf16[1536,768]{1,0:T(8,128)(2,1)}, u32[]{:S(2)}) copy-start(bf16[1536,768]{1,0:T(8,128)(2,1)} %get-tuple-element.66) | copy-start | bytes 7077892
  672.3 104.6 %copy-start.105 = (f32[96]{0:T(128)}, f32[96]{0:T(128)S(1)}, u32[]{:S(2)}) copy-start(f32[96]{0:T(128)S(1)} %dynamic-slice.11) | copy-start | bytes 1156
  (72 other events, 282.7 us)
Sparse Core Ops, SparseCore 0:
  10.0 26.7 all-gather.2
  38.7 24.1 all-gather.4
  260.9 35.3 reduce-scatter.12
  313.0 327.5 all-reduce.20
  644.4 39.2 reduce-scatter.6
  687.8 42.4 reduce-scatter.8
  734.3 42.4 reduce-scatter.10
where the time goes:
time: 791 us; the launch traced here: 785 us
  waiting for transfers between devices  357 us (45%)
  matrix products  216 us (27%)
  blocking collectives  93.9 us (12%)
  local copies, waits for them, and re-layouts  57 us (7%)
  other arithmetic  41.6 us (5%)
  between operations  19.2 us (2%)
    psum x1, waiting for transfers between devices, body(): lax.psum(branches.astype(jnp.bfloat16), 'tensor').astype(jnp.float32)  268 us
    unnamed x2, blocking collectives  49 us
    reduce_scatter x1, waiting for transfers between devices, body(): lax.psum_scatter(totals[6], 'dp', scatter_dimension=1, tiled=True)  46.4 us
    dot_general x8, matrix products, contract_cols(): lax.dot_general(left, right, (((1,), (1,)), ((), ())), preferred_element_...  44 us
    reduce_scatter x1, waiting for transfers between devices, body(): lax.psum_scatter(totals[4], 'dp', scatter_dimension=0, tiled=True)  40.7 us
    dot_general x8, matrix products, contract_rows(): lax.dot_general(left, right, (((0,), (0,)), ((), ())), preferred_element_...  34.1 us
    dot_general x2, matrix products, local_backward(): jnp.einsum('chst,csha->ctha', d_scores, query, preferred_element_type=jnp...  29.9 us
    dot_general x2, matrix products, local_forward(): jnp.dot(second_normed, up_full, preferred_element_type=jnp.float32)  29.6 us
  transfers between devices with their start and end apart: 7, of which 3 were waited for; matrix products, arithmetic and copies ran while one was open for 27% of the time, Pallas kernels for 0%

commit v1 on v0

v1 whole, which is shorter than its diff:
```python
import math

import jax
import jax.numpy as jnp
import numpy as np
from jax import lax
from jax.experimental import pallas as pl
from jax.experimental.pallas import tpu as pltpu
from jax.sharding import PartitionSpec as P

HD = 64
ROT = 16
SEQ = 512
EPS = 1e-05
VMEM = 56 * 1024 * 1024
F32 = jnp.float32
BF16 = jnp.bfloat16


def dot(left, right, left_dim, right_dim):
    return lax.dot_general(
        left, right, (((left_dim,), (right_dim,)), ((), ())), preferred_element_type=F32
    )


def normalise(values):
    average = jnp.mean(values, axis=-1, keepdims=True)
    centred = values - average
    spread = jnp.mean(centred * centred, axis=-1, keepdims=True)
    scale = lax.rsqrt(spread + EPS)
    return centred * scale, scale


def norm_back(d, hat, scale, gain):
    dg = d * gain
    first = jnp.mean(dg, axis=-1, keepdims=True)
    second = jnp.mean(dg * hat, axis=-1, keepdims=True)
    return (dg - first - hat * second) * scale


def rotary_tables():
    half = ROT // 2
    rates = 10000.0 ** (-(2.0 * np.arange(half)) / ROT)
    angles = rates[:, None] * np.arange(SEQ)[None, :]
    return np.cos(angles).astype(np.float32), np.sin(angles).astype(np.float32)


def rotate(values, cosine, sine):
    half = ROT // 2
    first, second = values[:half], values[half:ROT]
    return jnp.concatenate(
        [first * cosine - second * sine, second * cosine + first * sine, values[ROT:]], axis=0
    )


def attention_kernel(
    place, x_ref, g_ref, wt_ref, merge_ref, bias_ref, ln_ref, cos_ref, sin_ref,
    out_ref, din_ref, n1t_ref, gt_ref, dmh_ref, atth_ref, rows_ref, hb_ref,
    mixed, datt, att, dmix,
):
    groups = wt_ref.shape[0] // (9 * HD)
    rows = 9 * HD
    half = SEQ // 2
    scaling = 1.0 / math.sqrt(HD)
    x = x_ref[...].astype(F32)
    g = g_ref[...]
    gain, shift = ln_ref[0:1, :], ln_ref[1:2, :]
    hat, scale = normalise(x)
    n1 = (hat * gain + shift).astype(BF16)
    n1t_ref[0] = n1.T
    gt_ref[0] = g.T
    datt[...] = dot(merge_ref[...], g, 1, 1).astype(BF16)
    cosine, sine = cos_ref[...], sin_ref[...]
    below = lax.broadcasted_iota(jnp.int32, (half, half), 0) <= lax.broadcasted_iota(
        jnp.int32, (half, half), 1
    )

    def softmax(scores):
        top = jnp.max(scores, axis=0, keepdims=True)
        raised = jnp.exp(scores - top)
        return raised * (1.0 / jnp.sum(raised, axis=0, keepdims=True))

    def group(index, carry):
        base = pl.multiple_of(index * rows, rows)
        part = dot(wt_ref[pl.ds(base, rows), :], n1, 1, 1)
        bias = bias_ref[pl.ds(base, rows), :]
        part = part + jnp.concatenate([bias] * (SEQ // 128), axis=1)
        for head in range(3):
            at = head * 3 * HD
            query = rotate(part[at : at + HD], cosine, sine).astype(BF16)
            keys = rotate(part[at + HD : at + 2 * HD], cosine, sine).astype(BF16)
            values = part[at + 2 * HD : at + 3 * HD].astype(BF16)
            spot = pl.multiple_of(index * 3 * HD + head * HD, HD)
            given = datt[pl.ds(spot, HD), :]
            keys_t, values_t = keys.T, values.T
            s0 = dot(keys_t[:half], query[:, :half], 1, 0) * scaling
            s1a = dot(keys_t[:half], query[:, half:], 1, 0) * scaling
            s1b = dot(keys_t[half:], query[:, half:], 1, 0) * scaling
            s0 = jnp.where(below, s0, -1e30)
            s1b = jnp.where(below, s1b, -1e30)
            p0 = softmax(s0)
            p1 = softmax(jnp.concatenate([s1a, s1b], axis=0))
            w0, w1 = p0.astype(BF16), p1.astype(BF16)
            attended = jnp.concatenate(
                [dot(values[:, :half], w0, 1, 0), dot(values, w1, 1, 0)], axis=1
            )
            att[pl.ds(spot, HD), :] = attended.astype(BF16)
            q0 = dot(values_t[:half], given[:, :half], 1, 0)
            q1 = dot(values_t, given[:, half:], 1, 0)
            d0 = (p0 * (q0 - jnp.sum(q0 * p0, axis=0, keepdims=True)) * scaling).astype(BF16)
            d1 = (p1 * (q1 - jnp.sum(q1 * p1, axis=0, keepdims=True)) * scaling).astype(BF16)
            d_values = dot(given[:, half:], w1, 1, 1)
            d_values = jnp.concatenate(
                [d_values[:, :half] + dot(given[:, :half], w0, 1, 1), d_values[:, half:]], axis=1
            )
            d_keys = dot(query[:, half:], d1, 1, 1)
            d_keys = jnp.concatenate(
                [d_keys[:, :half] + dot(query[:, :half], d0, 1, 1), d_keys[:, half:]], axis=1
            )
            d_query = jnp.concatenate(
                [dot(keys[:, :half], d0, 1, 0), dot(keys, d1, 1, 0)], axis=1
            )
            to = pl.multiple_of(base + at, HD)
            dmix[pl.ds(to, HD), :] = rotate(d_query, cosine, -sine).astype(BF16)
            dmix[pl.ds(to + HD, HD), :] = rotate(d_keys, cosine, -sine).astype(BF16)
            dmix[pl.ds(to + 2 * HD, HD), :] = d_values.astype(BF16)
        return carry

    lax.fori_loop(0, groups, group, 0)
    out_ref[...] = dot(att[...].T, merge_ref[...], 1, 0)
    d_first = dot(dmix[...].T, wt_ref[...], 1, 0)
    pair = place[1]
    mine = dmix[pl.ds(pl.multiple_of(pair * 2 * rows, 2 * rows), 2 * rows), :]
    dmh_ref[0] = mine
    atth_ref[0] = att[pl.ds(pl.multiple_of(pair * 6 * HD, 6 * HD), 6 * HD), :]
    hb_ref[0] = dot(jnp.ones((8, SEQ), BF16), mine, 1, 1)
    rows_ref[0] = jnp.concatenate(
        [
            jnp.sum(d_first * hat, axis=0, keepdims=True),
            jnp.sum(d_first, axis=0, keepdims=True),
            jnp.sum(g.astype(F32), axis=0, keepdims=True),
            jnp.zeros((5, x.shape[1]), F32),
        ],
        axis=0,
    )
    din_ref[...] = norm_back(d_first, hat, scale, gain)


def gelu_parts(h):
    near = 0.7071067811865476 * jnp.abs(h)
    below = 1.0 + 0.3275911 * near
    t = pl.reciprocal(below, approx=True)
    t = t * (2.0 - below * t)
    bell = jnp.exp(-0.5 * h * h)
    series = 1.061405429 * t - 1.453152027
    series = series * t + 1.421413741
    series = series * t - 0.284496736
    series = series * t + 0.254829592
    tail = 0.5 * series * t * bell
    phi = jnp.where(h >= 0, 1.0 - tail, tail)
    return h * phi, phi + h * bell * 0.3989422804014327


def feed_kernel(
    place, x_ref, g_ref, up_ref, down_ref, bias_ref, ln_ref, aout_ref, din_ref,
    out_ref, t_ref, n2t_ref, act_ref, dh_ref, rows_ref,
    n2, hat_s, scale_s, acc, dacc, sums,
):
    step = pl.program_id(1)
    pair = place[1]
    gain, shift = ln_ref[2:3, :], ln_ref[3:4, :]

    @pl.when(step == 0)
    def _():
        hat, scale = normalise(x_ref[...].astype(F32))
        hat_s[...] = hat
        scale_s[...] = jnp.broadcast_to(scale, scale_s.shape)
        n2[...] = (hat * gain + shift).astype(BF16)
        n2t_ref[0] = n2[...].T
        sums[...] = jnp.zeros_like(sums)
        acc[...] = x_ref[...].astype(F32) + aout_ref[...] + ln_ref[4:5, :]
        dacc[...] = jnp.zeros_like(dacc)

    up, down = up_ref[0], down_ref[0]
    h = dot(n2[...], up, 1, 0) + bias_ref[0, 0:1, :]
    activated, slope = gelu_parts(h)
    activated = activated.astype(BF16)
    d_hidden = (dot(g_ref[...], down, 1, 0) * slope).astype(BF16)
    acc[...] += dot(activated, down, 1, 1)
    dacc[...] += dot(d_hidden, up, 1, 1)

    @pl.when(step // 2 == pair)
    def _():
        act_ref[0] = activated
        dh_ref[0] = d_hidden
        sums[pl.ds(step % 2, 1), :] = jnp.sum(d_hidden.astype(F32), axis=0, keepdims=True)

    @pl.when(step == pl.num_programs(1) - 1)
    def _():
        d_second = dacc[...]
        hat = hat_s[...]
        out_ref[...] = acc[...].astype(BF16)
        total = norm_back(d_second, hat, scale_s[:, 0:1], gain) + din_ref[...]
        t_ref[...] = total.astype(BF16)
        rows_ref[0] = jnp.concatenate(
            [
                jnp.sum(d_second * hat, axis=0, keepdims=True),
                jnp.sum(d_second, axis=0, keepdims=True),
                sums[0:2, :],
                jnp.zeros((4, hat.shape[1]), F32),
            ],
            axis=0,
        )


def heads_grad_kernel(n1t_ref, gt_ref, dmh_ref, atth_ref, out_ref, acc):
    step = pl.program_id(0)
    width = dmh_ref.shape[1]

    @pl.when(step == 0)
    def _():
        acc[...] = jnp.zeros_like(acc)

    acc[:, :width] += dot(n1t_ref[0], dmh_ref[0], 1, 1)
    acc[:, width:] += dot(gt_ref[0], atth_ref[0], 1, 1)

    @pl.when(step == pl.num_programs(0) - 1)
    def _():
        out_ref[...] = acc[...].astype(BF16)


def feed_grad_kernel(n2t_ref, gt_ref, dh_ref, act_ref, small_ref, out_ref, acc):
    step = pl.program_id(0)
    width = dh_ref.shape[2]

    @pl.when(step == 0)
    def _():
        acc[...] = jnp.zeros_like(acc)

    acc[:, :width] += dot(n2t_ref[0], dh_ref[0], 1, 0)
    acc[:, width:] += dot(gt_ref[0], act_ref[0], 1, 0)

    @pl.when(step == pl.num_programs(0) - 1)
    def _():
        out_ref[:, : 2 * width] = acc[...].astype(BF16)
        out_ref[:, 2 * width :] = small_ref[...].astype(BF16)


def params(*kinds):
    return pltpu.CompilerParams(dimension_semantics=kinds, vmem_limit_bytes=VMEM)


def whole(shape):
    zeros = (0,) * len(shape)
    return pl.BlockSpec(shape, lambda *_: zeros)


def attention(place, x, g, wt, merge, bias, ln, cosine, sine, count):
    width = x.shape[1]
    rows = 9 * HD
    given = pl.BlockSpec((SEQ, width), lambda i, place: (place[0] + i, 0))
    taken = pl.BlockSpec((SEQ, width), lambda i, place: (i, 0))

    def per(a, b):
        return pl.BlockSpec((1, a, b), lambda i, place: (i, 0, 0))

    return pl.pallas_call(
        attention_kernel,
        grid_spec=pltpu.PrefetchScalarGridSpec(
            num_scalar_prefetch=1,
            grid=(count,),
            in_specs=[
                given, given, whole(wt.shape), whole(merge.shape), whole(bias.shape),
                whole(ln.shape), whole(cosine.shape), whole(sine.shape),
            ],
            out_specs=[
                taken, taken, per(width, SEQ), per(width, SEQ), per(2 * rows, SEQ),
                per(6 * HD, SEQ), per(8, width), per(8, 2 * rows),
            ],
            scratch_shapes=[
                pltpu.VMEM((8, 128), BF16),
                pltpu.VMEM((width, SEQ), BF16),
                pltpu.VMEM((width, SEQ), BF16),
                pltpu.VMEM((wt.shape[0], SEQ), BF16),
            ],
        ),
        out_shape=[
            jax.ShapeDtypeStruct((count * SEQ, width), F32),
            jax.ShapeDtypeStruct((count * SEQ, width), F32),
            jax.ShapeDtypeStruct((count, width, SEQ), BF16),
            jax.ShapeDtypeStruct((count, width, SEQ), BF16),
            jax.ShapeDtypeStruct((count, 2 * rows, SEQ), BF16),
            jax.ShapeDtypeStruct((count, 6 * HD, SEQ), BF16),
            jax.ShapeDtypeStruct((count, 8, width), F32),
            jax.ShapeDtypeStruct((count, 8, 2 * rows), F32),
        ],
        compiler_params=params("arbitrary"),
        name="attention",
        cost_estimate=pl.CostEstimate(
            flops=count * 20_000_000_000, bytes_accessed=count * 12_000_000, transcendentals=0
        ),
    )(place, x, g, wt, merge, bias, ln, cosine, sine)


def feed(place, x, g, up, down, bias, ln, aout, din, count):
    width = x.shape[1]
    groups, _, ff = up.shape
    given = pl.BlockSpec((SEQ, width), lambda i, t, place: (place[0] + i, 0))
    taken = pl.BlockSpec((SEQ, width), lambda i, t, place: (i, 0))
    weight = pl.BlockSpec((1, width, ff), lambda i, t, place: (t, 0, 0))
    kept = pl.BlockSpec(
        (1, SEQ, ff), lambda i, t, place: (i, 0, jnp.clip(t - 2 * place[1], 0, 1))
    )
    return pl.pallas_call(
        feed_kernel,
        grid_spec=pltpu.PrefetchScalarGridSpec(
            num_scalar_prefetch=1,
            grid=(count, groups),
            in_specs=[
                given, given, weight, weight,
                pl.BlockSpec((1, 1, ff), lambda i, t, place: (t, 0, 0)),
                whole(ln.shape), taken, taken,
            ],
            out_specs=[
                taken, taken,
                pl.BlockSpec((1, width, SEQ), lambda i, t, place: (i, 0, 0)),
                kept, kept,
                pl.BlockSpec((1, 8, width), lambda i, t, place: (i, 0, 0)),
            ],
            scratch_shapes=[
                pltpu.VMEM((SEQ, width), BF16),
                pltpu.VMEM((SEQ, width), F32),
                pltpu.VMEM((SEQ, 128), F32),
                pltpu.VMEM((SEQ, width), F32),
                pltpu.VMEM((SEQ, width), F32),
                pltpu.VMEM((8, ff), F32),
            ],
        ),
        out_shape=[
            jax.ShapeDtypeStruct((count * SEQ, width), BF16),
            jax.ShapeDtypeStruct((count * SEQ, width), BF16),
            jax.ShapeDtypeStruct((count, width, SEQ), BF16),
            jax.ShapeDtypeStruct((count, SEQ, 2 * ff), BF16),
            jax.ShapeDtypeStruct((count, SEQ, 2 * ff), BF16),
            jax.ShapeDtypeStruct((count, 8, width), F32),
        ],
        compiler_params=params("arbitrary", "arbitrary"),
        name="feed",
        cost_estimate=pl.CostEstimate(
            flops=count * 15_000_000_000, bytes_accessed=count * 18_000_000, transcendentals=0
        ),
    )(place, x, g, up, down, bias, ln, aout, din)


def heads_grad(n1t, gt, dmh, atth):
    count, width, _ = n1t.shape
    columns = dmh.shape[1] + atth.shape[1]

    def per(array):
        return pl.BlockSpec((1,) + array.shape[1:], lambda i: (i, 0, 0))

    return pl.pallas_call(
        heads_grad_kernel,
        grid=(count,),
        in_specs=[per(n1t), per(gt), per(dmh), per(atth)],
        out_specs=whole((width, columns)),
        out_shape=jax.ShapeDtypeStruct((width, columns), BF16),
        scratch_shapes=[pltpu.VMEM((width, columns), F32)],
        compiler_params=params("arbitrary"),
        name="heads_grad",
        cost_estimate=pl.CostEstimate(
            flops=2 * count * SEQ * width * columns, bytes_accessed=8_000_000, transcendentals=0
        ),
    )(n1t, gt, dmh, atth)


def feed_grad(n2t, gt, dh, act, small):
    count, width, _ = n2t.shape
    columns = 2 * dh.shape[2]

    def per(array):
        return pl.BlockSpec((1,) + array.shape[1:], lambda i: (i, 0, 0))

    return pl.pallas_call(
        feed_grad_kernel,
        grid=(count,),
        in_specs=[per(n2t), per(gt), per(dh), per(act), whole(small.shape)],
        out_specs=whole((width, columns + small.shape[1])),
        out_shape=jax.ShapeDtypeStruct((width, columns + small.shape[1]), BF16),
        scratch_shapes=[pltpu.VMEM((width, columns), F32)],
        compiler_params=params("arbitrary"),
        name="feed_grad",
        cost_estimate=pl.CostEstimate(
            flops=2 * count * SEQ * width * columns, bytes_accessed=18_000_000, transcendentals=0
        ),
    )(n2t, gt, dh, act, small)


def body(
    block_input, cotangent, heads_weight, heads_bias, merge_weight, merge_bias, up_weight, up_bias,
    down_weight, down_bias, first_gain, first_shift, second_gain, second_shift,
):
    chunk = heads_weight.shape[0]
    owners = lax.axis_size("dp")
    groups = lax.axis_size("tensor")
    width = block_input.shape[1]
    spot = lax.axis_index("tensor")
    odd, pair = spot % 2, spot // 2
    total = block_input.shape[0] // SEQ
    count = total // 2
    place = jnp.stack([odd * count, pair]).astype(jnp.int32)

    bias_part = heads_bias.shape[0]
    vectors = jnp.stack(
        [
            jnp.pad(heads_bias, (0, chunk - bias_part)), up_bias, merge_bias, down_bias,
            first_gain, first_shift, second_gain, second_shift,
        ],
        axis=1,
    )
    early = jnp.concatenate(
        [heads_weight, merge_weight.T, jnp.pad(vectors, ((0, 0), (0, 120)))], axis=1
    )
    late = jnp.concatenate([up_weight, down_weight.T], axis=1)
    early = lax.all_gather(lax.all_gather(early, "dp", axis=0, tiled=True), "tensor", axis=0)
    late = lax.all_gather(lax.all_gather(late, "dp", axis=0, tiled=True), "tensor", axis=0)
    rows = 9 * HD
    wt = early[:, :, :rows].transpose(0, 2, 1).reshape(groups * rows, width)
    merge = early[:, :, rows : rows + 3 * HD].transpose(0, 2, 1).reshape(groups * 3 * HD, width)
    vecs = early[:, :, rows + 3 * HD : rows + 3 * HD + 8].astype(F32).transpose(0, 2, 1)
    hbias = vecs[:, 0].reshape(groups, owners, chunk)[:, :, :bias_part].reshape(groups * rows, 1)
    hbias = jnp.broadcast_to(hbias, (groups * rows, 128))
    ubias = vecs[:, 1:2, :]
    ln = jnp.concatenate(
        [vecs[0, 4:8], (vecs[0, 2] + vecs[0, 3])[None], jnp.zeros((3, width), F32)], axis=0
    )
    ff = up_weight.shape[1]
    up, down = late[:, :, :ff], late[:, :, ff:]

    cosine, sine = rotary_tables()
    aout, din, n1t, gt, dmh, atth, rows_a, hb = attention(
        place, block_input, cotangent, wt, merge, hbias, ln, cosine, sine, count
    )
    out16, t16, n2t, act, dh, rows_f = feed(
        place, block_input, cotangent, up, down, ubias, ln, aout, din, count
    )
    swap = [(i, i ^ 1) for i in range(groups)]
    out_other = lax.ppermute(out16, "tensor", swap)
    t_other = lax.ppermute(t16, "tensor", swap)

    first_cols = heads_grad(n1t, gt, dmh, atth)
    rows_a, rows_f, hb = rows_a.sum(0), rows_f.sum(0), hb.sum(0)[0]
    hb = jnp.pad(hb.reshape(2, owners, bias_part), ((0, 0), (0, 0), (0, chunk - bias_part)))
    small = jnp.concatenate(
        [rows_a[0:2], rows_f[0:2], rows_a[2:3], rows_f[2:4], hb.reshape(2, width)], axis=0
    )
    small = jnp.pad(small.T, ((0, 0), (0, 128 - 9)))
    second_cols = feed_grad(n2t, gt, dh, act, small)

    first_cols = lax.psum_scatter(first_cols, "dp", scatter_dimension=0, tiled=True)
    second_cols = lax.psum_scatter(second_cols, "dp", scatter_dimension=0, tiled=True)
    hw = first_cols[:, : 2 * rows].reshape(chunk, 2, rows)
    mw = first_cols[:, 2 * rows :].reshape(chunk, 2, 3 * HD)
    uw = second_cols[:, : 2 * ff].reshape(chunk, 2, ff)
    dw = second_cols[:, 2 * ff : 4 * ff].reshape(chunk, 2, ff)
    tiny = second_cols[:, 4 * ff :]
    halves = [
        jnp.concatenate(
            [hw[:, k], mw[:, k], uw[:, k], dw[:, k], tiny[:, 0:5], tiny[:, 5 + k : 6 + k], tiny[:, 7 + k : 8 + k]],
            axis=1,
        )
        for k in range(2)
    ]
    mine = jnp.where(odd == 0, halves[0], halves[1])
    other = jnp.where(odd == 0, halves[1], halves[0])
    full = mine.astype(F32) + lax.ppermute(other, "tensor", swap).astype(F32)
    a, b, c, d = rows, rows + 3 * HD, rows + 3 * HD + ff, rows + 3 * HD + 2 * ff

    layer_output = jnp.where(
        odd == 0,
        jnp.concatenate([out16, out_other], axis=0),
        jnp.concatenate([out_other, out16], axis=0),
    )
    terms = jnp.where(
        odd == 0,
        jnp.concatenate([t16, t_other], axis=0),
        jnp.concatenate([t_other, t16], axis=0),
    )
    input_grad = terms.astype(F32) + cotangent.astype(F32)
    return (
        layer_output,
        input_grad,
        full[:, :a],
        full[:bias_part, d + 6],
        full[:, a:b].T,
        full[:, d + 4],
        full[:, b:c],
        full[:, d + 5],
        full[:, c:d].T,
        full[:, d + 4],
        full[:, d],
        full[:, d + 1],
        full[:, d + 2],
        full[:, d + 3],
    )


def solution(mesh):
    placed = (
        P("dp", None),
        P("dp", None),
        P("dp", "tensor"),
        P(("tensor", "dp")),
        P("tensor", "dp"),
        P("dp"),
        P("dp", "tensor"),
        P(("tensor", "dp")),
        P("tensor", "dp"),
        P("dp"),
        P("dp"),
        P("dp"),
        P("dp"),
        P("dp"),
    )
    return jax.shard_map(
        body,
        mesh=mesh,
        in_specs=placed,
        out_specs=placed,
        check_vma=False,
    )
```

time: 791 us -> 546 us (0.69)
  matrix products: 216 us -> 0 us
  Pallas kernels: 0 us -> 142 us
  blocking collectives: 93.9 us -> 0 us
  waiting for transfers between devices: 357 us -> 318 us
  other arithmetic: 41.6 us -> 23.5 us
  local copies, waits for them, and re-layouts: 57 us -> 45 us
    psum x1 -> x0, waiting for transfers between devices: 268 us -> none  [body(): lax.psum(branches.astype(jnp.bfloat16), 'tensor').astype(jnp.float32)]
    all_gather x2 -> x4, waiting for transfers between devices: 0.04 us -> 231 us  [the longest x1 103 us: body(): lax.all_gather(lax.all_gather(early, 'dp', axis=0, tiled=True), 'tensor',...]
    dot_general x34 -> x0, matrix products: 204 us -> none  [the longest x8 44 us: contract_cols(): lax.dot_general(left, right, (((1,), (1,)), ((), ())), preferred_element_...]
    pallas_call x0 -> x4, Pallas kernels: none -> 142 us  [the longest x1 65.2 us: attention(): pl.pallas_call(attention_kernel, grid_spec=pltpu.PrefetchScalarGridSpec(n...]
    reduce_scatter x3 -> x2, waiting for transfers between devices: 87.2 us -> 0.02 us  [the longest x1 0.02 us: body(): lax.psum_scatter(first_cols, 'dp', scatter_dimension=0, tiled=True)]
    ppermute x0 -> x3, waiting for transfers between devices: none -> 85.9 us  [the longest x1 48.9 us: body(): t_other = lax.ppermute(t16, 'tensor', swap)]
    unnamed x2 -> x0, blocking collectives: 49 us -> none
    psum x1 -> x0, blocking collectives: 23 us -> none  [body(): lax.psum(grads[8].astype(jnp.bfloat16), 'tensor').astype(jnp.float32)]
  transfers between devices with their start and end apart: 7 -> 9, of which waited for: 3 -> 7; matrix products, arithmetic and copies ran while one was open for 27% -> 11% of each run, Pallas kernels for 0% -> 26%
where the time goes in v1:
time: 546 us; the launch traced here: 545 us
  waiting for transfers between devices  318 us (58%)
  Pallas kernels  142 us (26%)
  local copies, waits for them, and re-layouts  45 us (8%)
  other arithmetic  23.5 us (4%)
  between operations  14.4 us (3%)
    all_gather x1, waiting for transfers between devices, body(): lax.all_gather(lax.all_gather(early, 'dp', axis=0, tiled=True), 'tensor',...  103 us
    all_gather x1, waiting for transfers between devices, body(): lax.all_gather(lax.all_gather(late, 'dp', axis=0, tiled=True), 'tensor',...  70.9 us
    pallas_call x1, Pallas kernels, attention(): pl.pallas_call(attention_kernel, grid_spec=pltpu.PrefetchScalarGridSpec(n...  65.2 us
    pallas_call x1, Pallas kernels, feed(): pl.pallas_call(feed_kernel, grid_spec=pltpu.PrefetchScalarGridSpec(num_sc...  54.3 us
    ppermute x1, waiting for transfers between devices, body(): t_other = lax.ppermute(t16, 'tensor', swap)  48.9 us
    ppermute x1, waiting for transfers between devices, body(): out_other = lax.ppermute(out16, 'tensor', swap)  33.9 us
    all_gather x1, waiting for transfers between devices, body(): lax.all_gather(late, 'dp', axis=0, tiled=True)  31.4 us
    all_gather x1, waiting for transfers between devices, body(): lax.all_gather(early, 'dp', axis=0, tiled=True)  25.9 us
  transfers between devices with their start and end apart: 9, of which 7 were waited for; matrix products, arithmetic and copies ran while one was open for 11% of the time, Pallas kernels for 26%

profile of v1, /device:TPU:0, one launch (start us, length us, event | category | flops | bytes accessed | tf_op | source)
XLA Modules:
  0.0 544.9 jit_solution(5790410764984208369)
XLA Ops:
  7.2 0.7 pad_bitcast_fusion
  7.9 0.8 stack.47
  8.7 0.1 copy.80
  8.8 0.9 copy.56
  9.7 1.7 fusion.1
  11.4 1.7 pad_maximum_fusion
  13.2 25.9 %all-gather.9.cloned.1.call-done = bf16[768,896]{1,0:T(8,128)(2,1)} async-done(((bf16[96,896]{1,0:T(8,128)(2,1)}), bf16[768,896]{1,0:T(8,128)(2,1)}) %all-gather.9.cloned.1.call-update) | async-done | bytes 1376272 | tf_op jit(solution)/shard_map/all_gather | solution.py:425
  39.2 31.4 %all-gather.7.cloned.1.call-done = bf16[768,1536]{1,0:T(8,128)(2,1)} async-done(((bf16[96,1536]{1,0:T(8,128)(2,1)}), bf16[768,1536]{1,0:T(8,128)(2,1)}) %all-gather.7.cloned.1.call-update) | async-done | bytes 2359312 | tf_op jit(solution)/shard_map/all_gather | solution.py:426
  70.7 0.1 pad.30.clone
  70.8 0.6 pad_add_fusion.place
  71.4 103.2 %all-gather.13.cloned.1.call-done = bf16[3072,896]{1,0:T(8,128)(2,1)} async-done(((bf16[768,896]{1,0:T(8,128)(2,1)}), bf16[3072,896]{1,0:T(8,128)(2,1)}) %all-gather.13.cloned.1.call-update) | async-done | bytes 5505040 | tf_op jit(solution)/shard_map/all_gather | solution.py:425
  174.6 1.2 slice.187
  175.8 0.2 copy.71
  176.0 0.6 slice_reduce_fusion.7
  176.7 0.1 reshape_squeeze.6
  176.8 0.1 broadcast_in_dim.12
  176.8 4.4 slice_bitcast_fusion
  181.2 6.4 %copy.59 = bf16[4,576,768]{2,1,0:T(8,128)(2,1)} copy(bf16[4,576,768]{1,2,0:T(8,128)(2,1)} %slice_bitcast_fusion) | data formatting | bytes 7077888 | tf_op jit(solution)/shard_map/transpose | solution.py:428
  187.6 2.6 slice_bitcast_fusion.1
  190.3 1.5 copy.60
  191.8 0.7 maximum_maximum_fusion.ln_ref
  192.5 1.4 broadcast_in_dim.13.bias_ref
  193.9 65.2 %attention.1 = (f32[1536,768]{1,0:T(8,128)}, f32[1536,768]{1,0:T(8,128)}, bf16[3,768,512]{2,1,0:T(8,128)(2,1)}, bf16[3,768,512]{2,1,0:T(8,128)(2,1)}, bf16[3,115...) custom-call(s32[2]{0:T(128)} %pad_add_fusion.place, ...), custom_call_target="tpu_custom_call" | custom-call | flops 60000002048 | bytes 36000000 | tf_op jit(solution)/shard_map/attention/pallas_call | solution.py:267
  259.1 0.9 reduce_sum.27
  260.0 0.9 reduce_sum.29
  261.0 0.1 reshape_squeeze.7
  261.1 0.1 reshape.73
  261.1 9.0 %heads_grad.1 = bf16[768,1536]{1,0:T(8,128)(2,1)} custom-call(bf16[3,768,512]{2,1,0:T(8,128)(2,1)} %get-tuple-element.32.n1t_ref, bf16[3,768,512]{2,1,0:T(8,128)(2,1)} %get-tuple-element.33.gt_ref, bf16[3,1152,512]{2,1,0:T(8,128)(2,1)} %get-tuple-element.34.dmh_ref, bf16[3,384,512]{2,1,0:T(8,128)(2,1)} %get-tuple-element.35.atth_ref), custom_call_target="tpu_custom_call" | custom-call | flops 3623878656 | bytes 8000000 | tf_op jit(solution)/shard_map/heads_grad/pallas_call | solution.py:362
  270.2 70.9 %all-gather.11.cloned.1.call-done = bf16[3072,1536]{1,0:T(8,128)(2,1)} async-done(((bf16[768,1536]{1,0:T(8,128)(2,1)}), bf16[3072,1536]{1,0:T(8,128)(2,1)}) %all-gather.11.cloned.1.call-update) | async-done | bytes 9437200 | tf_op jit(solution)/shard_map/all_gather | solution.py:426
  341.2 8.1 %fusion.3 = (bf16[4,768,768]{2,1,0:T(8,128)(2,1)}, bf16[4,768,768]{2,1,0:T(8,128)(2,1)}) fusion(bf16[4,768,1536]{2,1,0:T(8,128)(2,1)} %bitcast.49), kind=kLoop, calls=%fused_computation.37 | loop fusion | bytes 18874368 | tf_op jit(solution)/shard_map/slice | solution.py:438
  349.3 54.3 %feed.1 = (bf16[1536,768]{1,0:T(8,128)(2,1)}, bf16[1536,768]{1,0:T(8,128)(2,1)}, bf16[3,768,512]{2,1,0:T(8,128)(2,1)}, bf16[3,512,1536]{2,1,0:T(8,128)(2,1)}, bf...) custom-call(s32[2]{0:T(128)} %pad_add_fusion.place, bf16[3072,768]{1,0:T(8,128)(2,1)} %x_ref.3, ...), custom_call_target="tpu_custom_call" | custom-call | flops 44999999488 | bytes 54000000 | tf_op jit(solution)/shard_map/feed/pallas_call | solution.py:314
  403.6 0.9 reduce_sum.28
  404.5 0.2 concatenate.38
  404.7 0.2 copy.63
  404.8 0.8 pad.19.small_ref
  405.6 13.8 %feed_grad.1 = bf16[768,3200]{1,0:T(8,128)(2,1)} custom-call(bf16[3,768,512]{2,1,0:T(8,128)(2,1)} %get-tuple-element.36.n2t_ref, bf16[3,768,512]{2,1,0:T(8,128)(2,1)} %get-tuple-element.33.gt_ref, bf16[3,512,1536]{2,1,0:T(8,128)(2,1)} %get-tuple-element.37.dh_ref, bf16[3,512,1536]{2,1,0:T(8,128)(2,1)} %get-tuple-element.38.act_ref, f32[768,128]{1,0:T(8,128)} %pad.19.small_ref), custom_call_target="tpu_custom_call" | custom-call | flops 7247757312 | bytes 18000000 | tf_op jit(solution)/shard_map/feed_grad/pallas_call | solution.py:384
  419.6 1.1 slice.196
  420.7 0.3 reshape.71
  420.9 0.9 slice.198
  421.8 0.1 reshape.72
  421.9 0.1 fusion.9
  422.1 0.3 fusion.8
  422.5 0.7 copy_bitcast_fusion.4
  423.2 1.8 collective-permute-start
  425.0 48.9 %collective-permute-done.1 = bf16[1536,768]{1,0:T(8,128)(2,1)} collective-permute-done((bf16[1536,768]{1,0:T(8,128)(2,1)}, bf16[1536,768]{1,0:T(8,128)(2,1)}, u32[]{:S(2)}, u32[]{:S(2)}) %collective-permute-start.1) | collective-permute-done | bytes 2359328 | tf_op jit(solution)/shard_map/ppermute | solution.py:449
  473.9 9.9 %convert_add_fusion = f32[3072,768]{1,0:T(8,128)} fusion(bf16[3072,768]{1,0:T(8,128)(2,1)} %g_ref.3, bf16[1536,768]{1,0:T(8,128)(2,1)} %collective-permute-done.1, bf16[1536,768]{1,0:T(8,128)(2,1)} %get-tuple-element.31, pred[]{:T(512)S(6)} %eq.4), kind=kLoop, calls=%fused_computation | loop fusion | flops 28311552 | bytes 18874368 | tf_op jit(solution)/shard_map/add | solution.py:489
  483.9 1.1 fusion.5
  485.1 1.6 fusion.4
  486.7 0.4 fusion.7
  487.1 0.4 fusion.6
  487.6 0.7 copy_bitcast_fusion
  488.3 1.0 concatenate.39
  489.3 1.1 concatenate.40
  490.6 33.9 %collective-permute-done = bf16[1536,768]{1,0:T(8,128)(2,1)} collective-permute-done((bf16[1536,768]{1,0:T(8,128)(2,1)S(1)}, bf16[1536,768]{1,0:T(8,128)(2,1)}, u32[]{:S(2)}, u32[]{:S(2)}) %collective-permute-start) | collective-permute-done | bytes 2359328 | tf_op jit(solution)/shard_map/ppermute | solution.py:448
  524.5 5.9 %maximum_select_fusion = bf16[3072,768]{1,0:T(8,128)(2,1)} fusion(bf16[1536,768]{1,0:T(8,128)(2,1)} %collective-permute-done, bf16[1536,768]{1,0:T(8,128)(2,1)S(1)} %copy-done, pred[]{:T(512)S(6)} %eq.4), kind=kLoop, calls=%fused_computation.1 | loop fusion | flops 21233664 | bytes 9437185 | tf_op jit(solution)/shard_map/jit(_where)/select_n | solution.py:479
  530.4 3.0 collective-permute-done.2
  533.5 0.2 convert_add_fusion.1
  533.7 0.7 slice_reduce_fusion.6
  534.3 0.8 slice_reduce_fusion
  535.2 0.1 slice_bitcast_fusion.3
  535.2 0.7 slice.218
  536.0 0.8 slice_bitcast_fusion.2
  536.8 0.7 copy.70
  537.5 0.5 copy.90
  (41 shorter events, 0.9 us)
Async XLA Ops:
  7.2 31.9 %all-gather.9.cloned.1.call-start = ((), (), s32[]{:S(2)}) async-start(), calls=%async_computation.3 | async-start | bytes 1548288 | tf_op jit(solution)/shard_map/all_gather | solution.py:425
  11.4 59.2 %all-gather.7.cloned.1.call-start = ((), (), s32[]{:S(2)}) async-start(), calls=%async_computation.2 | async-start | bytes 2654208 | tf_op jit(solution)/shard_map/all_gather | solution.py:426
  13.2 161.4 %all-gather.13.cloned.1.call-start = ((), (), s32[]{:S(2)}) async-start(), calls=%async_computation.7 | async-start | bytes 6881280 | tf_op jit(solution)/shard_map/all_gather | solution.py:425
  39.1 302.0 %all-gather.11.cloned.1.call-start = ((), (), s32[]{:S(2)}) async-start(), calls=%async_computation.6 | async-start | bytes 11796480 | tf_op jit(solution)/shard_map/all_gather | solution.py:426
  70.6 348.9 %reduce-scatter.3.cloned.1.call-start = ((), (), s32[]{:S(2)}) async-start(), calls=%async_computation.4 | async-start | bytes 2654208 | tf_op jit(solution)/shard_map/reduce_scatter | solution.py:460
  260.0 10.1 %copy-start.1 = (f32[8,768]{1,0:T(8,128)}, f32[8,768]{1,0:T(8,128)S(1)}, u32[]{:S(2)}) copy-start(f32[8,768]{1,0:T(8,128)S(1)} %reduce_sum.27) | copy-start | bytes 73732
  270.2 213.7 %reduce-scatter.5.cloned.1.call-start = ((), (), s32[]{:S(2)}) async-start(), calls=%async_computation.5 | async-start | bytes 5529600 | tf_op jit(solution)/shard_map/reduce_scatter | solution.py:461
  349.3 55.2 %slice-start.2 = ((f32[8,768]{1,0:T(8,128)}), f32[2,768]{1,0:T(2,128)S(1)}, s32[]{:S(2)}) async-start(f32[8,768]{1,0:T(8,128)} %copy-done.1), calls=%async_computation.10 | async-start | bytes 12288 | tf_op jit(solution)/shard_map/slice | solution.py:455
  419.4 3.8 copy-start
  419.5 54.5 %collective-permute-start.1 = (bf16[1536,768]{1,0:T(8,128)(2,1)}, bf16[1536,768]{1,0:T(8,128)(2,1)}, u32[]{:S(2)}, u32[]{:S(2)}) collective-permute-start(bf16[1536,768]{1,0:T(8,128)(2,1)} %get-tuple-element.31), channel_id=1, source_target_pairs={{0,1},{1,0},{2,3},{3,2},{4,5},{5,4},{6,7},{7,6},{8,9},{9,8},{10,11... | collective-permute-start | bytes 7077896 | tf_op jit(solution)/shard_map/ppermute | solution.py:449
  423.2 101.3 %collective-permute-start = (bf16[1536,768]{1,0:T(8,128)(2,1)S(1)}, bf16[1536,768]{1,0:T(8,128)(2,1)}, u32[]{:S(2)}, u32[]{:S(2)}) collective-permute-start(bf16[1536,768]{1,0:T(8,128)(2,1)S(1)} %copy-done), channel_id=1, source_target_pairs={{0,1},{1,0},{2,3},{3,2},{4,5},{5,4},{6,7},{7,6},{8,9},{9,8},{10,11... | collective-permute-start | bytes 7077896 | tf_op jit(solution)/shard_map/ppermute | solution.py:448
  483.9 4.4 slice-start
  483.9 5.4 slice-start.1
  490.5 43.0 %collective-permute-start.2 = (bf16[96,2311]{1,0:T(8,128)(2,1)S(1)}, bf16[96,2311]{1,0:T(8,128)(2,1)S(1)}, u32[]{:S(2)}, u32[]{:S(2)}) collective-permute-start(bf16[96,2311]{1,0:T(8,128)(2,1)S(1)} %broadcast_select_fusion), channel_id=1, source_target_pairs={{0,1},{1,0},{2,3},{3,2},{4,5},{5,4},{6,7},{7,6},{8,9},{9,8},{10,11... | collective-permute-start | bytes 1331144 | tf_op jit(solution)/shard_map/ppermute | solution.py:476
  535.1 2.9 copy-start.2
Sparse Core Ops, SparseCore 0:
  11.5 27.5 all-gather.8
  41.5 29.0 all-gather.6
  72.2 102.3 all-gather.12
  176.0 165.1 all-gather.10
  344.4 40.6 reduce-scatter.2
  419.6 52.9 reduce-scatter.4
